TPU v7x, 512 devices: a whole 4x4x16 slice. The times are simulated.
512 devices in a mesh: grp: 16 (over z), tile: 8 (over x_hi, y), arch: 4 (over x_lo, core).
Axes of the slice: x: 4 (x_hi: 2, x_lo: 2; x = x_hi * 2 + x_lo), y: 4, z: 16, core: 2. Of those that a mesh axis runs over, the one named last changes fastest.
Arguments:
- query_grads: bfloat16 [4, 1536, 4096], P('arch', 'tile', 'grp'), may hold values from -6 to 6
- input_basis: bfloat16 [4096, 4096], P(None, 'grp'), may hold values from -0.09375 to 0.09375
- output_basis: bfloat16 [1536, 1536], P(None, 'tile'), may hold values from -0.15625 to 0.15625
- eigenvalues: float32 [1536, 4096], P('tile', 'grp'), may hold values from 0.1 to 10
- activations: bfloat16 [1024, 4096], P('arch', 'grp'), may hold values from -6 to 6
- gradients: bfloat16 [1024, 1536], P('arch', 'tile'), may hold values from -0.0099487305 to 0.0099487305
- seq_lengths: int32 [4, 8], P('arch'), may hold values from 1 to 128, 256 in all within a row
Outputs:
- preconditioned: bfloat16 [4, 4096, 1536], P('arch', 'grp', 'tile')
- sequence_scores: float32 [4, 32], P(None, 'arch')
Inputs may be any that keep to these rules, and one draw needn't show every extreme that they name: Each row of seq_lengths sums to 256, and its largest entry is exactly 128.
All inputs are finite; a program needn't handle non-finite values.
Results may differ from a plain program's by a relative error of at most 0.013.
Values may be sent and summed in bfloat16 or wider, within the bound.
A program may use at most 64 MiB of HBM per device.

v0:
```python
import jax
import jax.numpy as jnp
from jax import lax
from jax.sharding import PartitionSpec as P

damping = 0.01


def contract_first(left_side, right_side):
    return lax.dot_general(
        left_side, right_side, (((0,), (0,)), ((), ())), preferred_element_type=jnp.float32
    )


def contract_last(left_side, right_side):
    return lax.dot_general(
        left_side, right_side, (((1,), (1,)), ((), ())), preferred_element_type=jnp.float32
    )


def per_device(
    query_grads, input_basis, output_basis, eigenvalues, activations, gradients, seq_lengths
):
    local_query = query_grads[0]
    feat_rows = local_query.shape[0]
    input_cols = local_query.shape[1]
    basis_part = input_basis
    rotated_in = jnp.dot(
        lax.all_gather(local_query, "grp", axis=1, tiled=True),
        basis_part,
        preferred_element_type=jnp.float32,
    ).astype(jnp.bfloat16)
    basis_part = output_basis
    rotated = contract_first(basis_part, lax.all_gather(rotated_in, "tile", axis=0, tiled=True))
    scaled = (rotated / (eigenvalues + damping)).astype(jnp.bfloat16)
    basis_part = output_basis
    restored = lax.psum_scatter(
        jnp.dot(basis_part, scaled, preferred_element_type=jnp.float32).astype(jnp.bfloat16),
        "tile",
        scatter_dimension=0,
        tiled=True,
    )
    basis_part = input_basis
    summed = lax.psum_scatter(
        contract_last(basis_part, restored), "grp", scatter_dimension=0, tiled=True
    )
    preconditioned = summed.astype(jnp.bfloat16)
    all_queries = lax.all_gather(preconditioned[None], "arch", axis=0, tiled=True)
    query_count = all_queries.shape[0]
    stacked = jnp.transpose(all_queries, (1, 0, 2)).reshape(input_cols, query_count * feat_rows)
    projected = jnp.dot(activations, stacked, preferred_element_type=jnp.float32)
    projected = projected.reshape(activations.shape[0], query_count, feat_rows)
    partial_scores = jnp.sum(projected * gradients.astype(jnp.float32)[:, None, :], axis=2).T
    lengths = seq_lengths[0]
    ends = jnp.cumsum(lengths)
    starts = ends - lengths
    position = jnp.arange(activations.shape[0], dtype=jnp.int32)
    member = ((position[None, :] >= starts[:, None]) & (position[None, :] < ends[:, None])).astype(
        jnp.float32
    )
    seq_sizes = lengths.astype(jnp.float32)
    token_scores = lax.psum(partial_scores, ("grp", "tile"))
    totals = jnp.dot(token_scores, member.T, precision=lax.Precision.HIGHEST)
    sequence_scores = totals / seq_sizes[None, :]
    return (preconditioned[None], sequence_scores)


def solution(mesh):
    return jax.shard_map(
        per_device,
        mesh=mesh,
        in_specs=(
            P("arch", "tile", "grp"),
            P(None, "grp"),
            P(None, "tile"),
            P("tile", "grp"),
            P("arch", "grp"),
            P("arch", "tile"),
            P("arch", None),
        ),
        out_specs=(P("arch", "grp", "tile"), P(None, "arch")),
        check_vma=False,
    )
```

profile of v0, /device:TPU:2, one launch (start us, length us, event | category | flops | bytes accessed | tf_op | source)
XLA Modules:
  0.0 666.5 jit_solution(9814027762734079321)
XLA Ops:
  7.2 0.0 copy-start
  7.2 0.0 all-gather.4.cloned.1.call-start
  7.2 0.7 all-gather.4.cloned.1.call-update
  7.9 0.0 copy-start.1
  7.9 0.0 reduce-scatter.7.cloned.1.call-start
  8.0 82.4 %all-gather.4.cloned.1.call-done = bf16[1,192,4096]{2,1,0:T(8,128)(2,1)} async-done(((bf16[1,192,256]{2,1,0:T(8,128)(2,1)}), bf16[1,192,4096]{2,1,0:T(8,128)(2,1)}) %all-gather.4.cloned.1.call-update) | async-done | bytes 1572880 | tf_op jit(solution)/shard_map/all_gather | solution.py:29
  90.3 0.0 copy-done
  90.3 2.0 fusion.5
  92.3 35.8 %all_gather.10 = bf16[1536,256]{1,0:T(8,128)(2,1)S(1)} all-gather(bf16[192,256]{1,0:T(8,128)(2,1)S(1)} %fusion.5), channel_id=1, replica_groups=mesh['grp'=16,'tile'=8,'arch'=4] {'tile'}, dimensions={0}, use_global_device_ids=true | all-gather | bytes 884736 | tf_op jit(solution)/shard_map/all_gather | solution.py:34
  128.2 0.0 copy-done.1
  128.2 2.8 fusion
  131.0 2.3 copy.11
  133.3 0.0 reduce-scatter.7.cloned.1.call-update
  133.3 0.0 reduce-scatter.5.cloned.1.call-start
  133.3 81.0 %reduce-scatter.7.cloned.1.call-done = bf16[192,256]{1,0:T(8,128)(2,1)} async-done(((bf16[1536,256]{1,0:T(8,128)(2,1)}), bf16[192,256]{1,0:T(8,128)(2,1)}) %reduce-scatter.7.cloned.1.call-update) | async-done | bytes 98320
  214.3 3.4 convolution_bitcast_fusion
  217.7 0.0 copy-start.4
  217.7 0.0 copy-start.5
  217.7 0.0 copy-start.3
  217.7 0.0 reduce-scatter.5.cloned.1.call-update
  217.8 0.9 copy-done.4
  218.6 0.0 copy-done.5
  218.6 0.2 reduce-window.7
  218.8 75.6 %reduce-scatter.5.cloned.1.call-done = f32[256,192]{0,1:T(8,128)} async-done(((f32[4096,192]{0,1:T(8,128)}), f32[256,192]{0,1:T(8,128)}) %reduce-scatter.5.cloned.1.call-update) | async-done | bytes 196624 | tf_op jit(solution)/shard_map/reduce_scatter | solution.py:44
  294.4 0.0 copy-start.2
  294.4 1.0 convert_element_type.27
  295.4 6.1 all-gather.1
  301.6 0.0 copy-done.3
  301.6 0.3 fusion.15
  301.9 0.1 multiply_reduce_fusion
  302.0 356.6 %psum.7 = f32[4,256]{1,0:T(4,128)S(1)} all-reduce(f32[4,256]{1,0:T(4,128)S(1)} %bitcast.50), channel_id=1, replica_groups=mesh['grp'=16,'tile'=8,'arch'=4] {'grp','tile'}, use_global_device_ids=true, to_apply=%region_3.0 | all-reduce | flops 1024 | bytes 8192 | tf_op jit(solution)/shard_map/psum | solution.py:62
  658.6 0.8 convolution_divide_fusion
  659.4 0.0 copy-done.2
  659.4 0.7 convert_bitcast_fusion.1
  (4 shorter events, 0.0 us)
Async XLA Ops:
  7.2 83.2 %copy-start = (bf16[4096,256]{1,0:T(8,128)(2,1)S(1)}, bf16[4096,256]{1,0:T(8,128)(2,1)}, u32[]{:S(2)}) copy-start(bf16[4096,256]{1,0:T(8,128)(2,1)} %param.8) | copy-start | bytes 6291460
  7.2 83.2 %all-gather.4.cloned.1.call-start = ((), (), s32[]{:S(2)}) async-start(), calls=%async_computation.3 | async-start | bytes 1671168 | tf_op jit(solution)/shard_map/all_gather | solution.py:29
  7.9 120.3 %copy-start.1 = (bf16[1536,192]{0,1:T(8,128)(2,1)S(1)}, bf16[1536,192]{0,1:T(8,128)(2,1)}, u32[]{:S(2)}) copy-start(bf16[1536,192]{0,1:T(8,128)(2,1)} %param.9) | copy-start | bytes 1769476
  7.9 206.4 %reduce-scatter.7.cloned.1.call-start = ((), (), s32[]{:S(2)}) async-start(), calls=%async_computation.4 | async-start | bytes 884736
  133.3 161.1 %reduce-scatter.5.cloned.1.call-start = ((), (), s32[]{:S(2)}) async-start(), calls=%async_computation.2 | async-start | bytes 3342336 | tf_op jit(solution)/shard_map/reduce_scatter | solution.py:44
  217.7 0.9 copy-start.4
  217.7 0.9 copy-start.5
  217.7 83.9 %copy-start.3 = (bf16[256,256]{1,0:T(8,128)(2,1)S(1)}, bf16[256,256]{1,0:T(8,128)(2,1)}, u32[]{:S(2)}) copy-start(bf16[256,256]{1,0:T(8,128)(2,1)} %param.11) | copy-start | bytes 393220
  294.4 364.9 %copy-start.2 = (f32[256,192]{0,1:T(8,128)S(1)}, f32[256,192]{0,1:T(8,128)}, u32[]{:S(2)}) copy-start(f32[256,192]{0,1:T(8,128)} %reduce-scatter.5.cloned.1.call-done) | copy-start | bytes 589828
Sparse Core Ops, SparseCore 0:
  10.0 80.2 all-gather.3
  133.4 80.8 reduce-scatter.6
  217.9 76.5 reduce-scatter.4
where the time goes:
time: 667 us
  blocking collectives  399 us (60%)
  waiting for transfers between devices  240 us (36%)
  between operations  13.8 us (2%)
  matrix products  9.26 us (1%)
    psum x1, blocking collectives, per_device(): token_scores = lax.psum(partial_scores, ('grp', 'tile'))  357 us
    all_gather x1, waiting for transfers between devices, per_device(): lax.all_gather(local_query, 'grp', axis=1, tiled=True)  82.4 us
    unnamed x4, waiting for transfers between devices  81.7 us
    reduce_scatter x1, waiting for transfers between devices, per_device(): lax.psum_scatter(contract_last(basis_part, restored), 'grp', scatter_dime...  75.6 us
    all_gather x1, blocking collectives, per_device(): lax.all_gather(rotated_in, 'tile', axis=0, tiled=True)  35.8 us
  transfers between devices with their start and end apart: 3, of which 3 were waited for; matrix products, arithmetic and copies ran while one was open for 0% of the time, Pallas kernels for 0%

commit v1 on v0

--- a/solution.py
+++ b/solution.py
@@ -31,7 +31,12 @@
         preferred_element_type=jnp.float32,
     ).astype(jnp.bfloat16)
     basis_part = output_basis
-    rotated = contract_first(basis_part, lax.all_gather(rotated_in, "tile", axis=0, tiled=True))
+    rotated = contract_first(
+        basis_part,
+        jnp.concatenate(
+            lax.all_to_all(jnp.stack([rotated_in] * lax.axis_size("tile")), "tile", 0, 0), axis=0
+        ),
+    )
     scaled = (rotated / (eigenvalues + damping)).astype(jnp.bfloat16)
     basis_part = output_basis
     restored = lax.psum_scatter(

time: 667 us -> 646 us (0.969)
  blocking collectives: 399 us -> 380 us
    all_gather x1 -> x0, blocking collectives: 35.8 us -> none  [per_device(): lax.all_gather(rotated_in, 'tile', axis=0, tiled=True)]
    all_to_all x0 -> x1, blocking collectives: none -> 17.3 us  [per_device(): lax.all_to_all(jnp.stack([rotated_in] * lax.axis_size('tile')), 'tile', 0...]
where the time goes in v1:
time: 646 us
  blocking collectives  380 us (59%)
  waiting for transfers between devices  237 us (37%)
  between operations  13.8 us (2%)
  matrix products  9.25 us (1%)
    psum x1, blocking collectives, per_device(): token_scores = lax.psum(partial_scores, ('grp', 'tile'))  357 us
    all_gather x1, waiting for transfers between devices, per_device(): lax.all_gather(local_query, 'grp', axis=1, tiled=True)  82.4 us
    unnamed x4, waiting for transfers between devices  79.5 us
    reduce_scatter x1, waiting for transfers between devices, per_device(): lax.psum_scatter(contract_last(basis_part, restored), 'grp', scatter_dime...  75.6 us
    all_to_all x1, blocking collectives, per_device(): lax.all_to_all(jnp.stack([rotated_in] * lax.axis_size('tile')), 'tile', 0...  17.3 us
  transfers between devices with their start and end apart: 3, of which 3 were waited for; matrix products, arithmetic and copies ran while one was open for 0% of the time, Pallas kernels for 0%

profile of v1, /device:TPU:2, one launch (start us, length us, event | category | flops | bytes accessed | tf_op | source)
XLA Modules:
  0.0 645.8 jit_solution(7211514852967362373)
XLA Ops:
  7.2 0.0 copy-start
  7.2 0.0 all-gather.4.cloned.1.call-start
  7.2 0.7 all-gather.4.cloned.1.call-update
  7.9 0.0 reduce-scatter.7.cloned.1.call-start
  8.0 82.4 %all-gather.4.cloned.1.call-done = bf16[1,192,4096]{2,1,0:T(8,128)(2,1)} async-done(((bf16[1,192,256]{2,1,0:T(8,128)(2,1)}), bf16[1,192,4096]{2,1,0:T(8,128)(2,1)}) %all-gather.4.cloned.1.call-update) | async-done | bytes 1572880 | tf_op jit(solution)/shard_map/all_gather | solution.py:29
  90.3 0.0 copy-done
  90.3 2.0 fusion.5
  92.3 0.0 copy-start.1
  92.3 0.1 stack.2
  92.4 17.3 %all_to_all.5 = bf16[8,192,256]{2,1,0:T(8,128)(2,1)S(1)} all-to-all(bf16[8,192,256]{2,1,0:T(8,128)(2,1)S(1)} %stack.2), channel_id=1, replica_groups=mesh['grp'=16,'tile'=8,'arch'=4] {'tile'}, dimensions={0} | all-to-all | bytes 1572864 | tf_op jit(solution)/shard_map/all_to_all | solution.py:37
  109.7 0.0 copy-done.1
  109.7 2.8 fusion
  112.5 2.3 copy.11
  114.8 0.0 reduce-scatter.7.cloned.1.call-update
  114.8 0.0 reduce-scatter.5.cloned.1.call-start
  114.9 78.8 %reduce-scatter.7.cloned.1.call-done = bf16[192,256]{1,0:T(8,128)(2,1)} async-done(((bf16[1536,256]{1,0:T(8,128)(2,1)}), bf16[192,256]{1,0:T(8,128)(2,1)}) %reduce-scatter.7.cloned.1.call-update) | async-done | bytes 98320
  193.6 3.4 convolution_bitcast_fusion
  197.0 0.0 copy-start.4
  197.0 0.0 copy-start.5
  197.0 0.0 copy-start.3
  197.0 0.0 reduce-scatter.5.cloned.1.call-update
  197.0 0.9 copy-done.4
  197.9 0.0 copy-done.5
  197.9 0.2 reduce-window.7
  198.1 75.6 %reduce-scatter.5.cloned.1.call-done = f32[256,192]{0,1:T(8,128)} async-done(((f32[4096,192]{0,1:T(8,128)}), f32[256,192]{0,1:T(8,128)}) %reduce-scatter.5.cloned.1.call-update) | async-done | bytes 196624 | tf_op jit(solution)/shard_map/reduce_scatter | solution.py:49
  273.7 0.0 copy-start.2
  273.7 1.0 convert_element_type.27
  274.7 6.1 all-gather.1
  280.9 0.0 copy-done.3
  280.9 0.3 fusion.15
  281.2 0.1 multiply_reduce_fusion
  281.3 356.6 %psum.7 = f32[4,256]{1,0:T(4,128)S(1)} all-reduce(f32[4,256]{1,0:T(4,128)S(1)} %bitcast.52), channel_id=1, replica_groups=mesh['grp'=16,'tile'=8,'arch'=4] {'grp','tile'}, use_global_device_ids=true, to_apply=%region_3.0 | all-reduce | flops 1024 | bytes 8192 | tf_op jit(solution)/shard_map/psum | solution.py:67
  637.9 0.8 convolution_divide_fusion
  638.6 0.0 copy-done.2
  638.6 0.7 convert_bitcast_fusion.1
  (4 shorter events, 0.0 us)
Async XLA Ops:
  7.2 83.2 %copy-start = (bf16[4096,256]{1,0:T(8,128)(2,1)S(1)}, bf16[4096,256]{1,0:T(8,128)(2,1)}, u32[]{:S(2)}) copy-start(bf16[4096,256]{1,0:T(8,128)(2,1)} %param.8) | copy-start | bytes 6291460
  7.2 83.2 %all-gather.4.cloned.1.call-start = ((), (), s32[]{:S(2)}) async-start(), calls=%async_computation.4 | async-start | bytes 1671168 | tf_op jit(solution)/shard_map/all_gather | solution.py:29
  7.9 185.7 %reduce-scatter.7.cloned.1.call-start = ((), (), s32[]{:S(2)}) async-start(), calls=%async_computation.5 | async-start | bytes 884736
  92.3 17.3 %copy-start.1 = (bf16[1536,192]{0,1:T(8,128)(2,1)S(1)}, bf16[1536,192]{0,1:T(8,128)(2,1)}, u32[]{:S(2)}) copy-start(bf16[1536,192]{0,1:T(8,128)(2,1)} %param.9) | copy-start | bytes 1769476
  114.8 158.9 %reduce-scatter.5.cloned.1.call-start = ((), (), s32[]{:S(2)}) async-start(), calls=%async_computation.3 | async-start | bytes 3342336 | tf_op jit(solution)/shard_map/reduce_scatter | solution.py:49
  197.0 0.9 copy-start.4
  197.0 0.9 copy-start.5
  197.0 83.9 %copy-start.3 = (bf16[256,256]{1,0:T(8,128)(2,1)S(1)}, bf16[256,256]{1,0:T(8,128)(2,1)}, u32[]{:S(2)}) copy-start(bf16[256,256]{1,0:T(8,128)(2,1)} %param.11) | copy-start | bytes 393220
  273.7 364.9 %copy-start.2 = (f32[256,192]{0,1:T(8,128)S(1)}, f32[256,192]{0,1:T(8,128)}, u32[]{:S(2)}) copy-start(f32[256,192]{0,1:T(8,128)} %reduce-scatter.5.cloned.1.call-done) | copy-start | bytes 589828
Sparse Core Ops, SparseCore 0:
  10.0 80.2 all-gather.3
  114.9 78.6 reduce-scatter.6
  197.2 76.5 reduce-scatter.4
